TPU v7x, 128 devices: a whole 4x4x4 slice. The times are simulated.
128 devices in a mesh: grp: 2 (over core), dev: 64 (over x, y, z).
Axes of the slice: x: 4, y: 4, z: 4, core: 2. Of those that a mesh axis runs over, the one named last changes fastest.
Arguments:
- tokens: bfloat16 [8192, 4096], P('dev'), may hold values from -6 to 6
- experts: int32 [8192, 8], P('dev'), may hold values from 0 to 63, all different within a row; in each aligned block of 128 rows (0 to 127, 128 to 255, ...) at most 24 rows name the same one
- gate_weight: float32 [8192, 8], P('dev'), may hold values from 0.1 to 1
- w_gate: bfloat16 [64, 4096, 1536], P('dev', None, 'grp'), may hold values from -0.09375 to 0.09375
- w_up: bfloat16 [64, 4096, 1536], P('dev', None, 'grp'), may hold values from -0.09375 to 0.09375
- w_down: bfloat16 [64, 1536, 4096], P('dev', 'grp'), may hold values from -0.15625 to 0.15625
Outputs:
- mixed: bfloat16 [8192, 4096], P('dev')
Inputs may be any that keep to these rules, and one draw needn't show every extreme that they name: In each aligned block of 128 tokens (the tokens of one index of dev) no expert is chosen more than 24 times, a bound that some block reaches; a token's 8 experts differ.
All inputs are finite; a program needn't handle non-finite values.
Results may differ from a plain program's by a relative error of at most 0.0065.
Values may be sent and summed in bfloat16 or wider, within the bound.
No kernel may reach another device: no remote copies, remote signals or barrier semaphores. Data moves between devices by JAX's collectives and lax.ppermute only.
A program may use at most 128 MiB of HBM per device.

v0:
```python
import jax
import jax.numpy as jnp
from jax import lax
from jax.sharding import PartitionSpec as P


def per_device(tokens, experts, gate_weight, w_gate, w_up, w_down):
    tok_rows, feat_width = tokens.shape
    top_count = experts.shape[1]
    n_experts = lax.axis_size("dev")
    slot_cap = 3 * tok_rows * top_count // (2 * n_experts)
    flat_ids = experts.reshape(-1)
    onehot = (flat_ids[:, None] == jnp.arange(n_experts, dtype=jnp.int32)[None, :]).astype(
        jnp.int32
    )
    ranks = jnp.cumsum(onehot, axis=0) - 1
    within = jnp.sum(ranks * onehot, axis=1)
    slot_index = flat_ids * slot_cap + within
    src_rows = jnp.arange(tok_rows * top_count, dtype=jnp.int32) // top_count
    table = jnp.full((n_experts * slot_cap,), tok_rows, jnp.int32).at[slot_index].set(src_rows)
    padded = jnp.concatenate([tokens, jnp.zeros((1, feat_width), tokens.dtype)], axis=0)
    send_buffer = padded[table].reshape(n_experts, slot_cap, feat_width)
    gate_mat = w_gate[0]
    up_mat = w_up[0]
    down_mat = w_down[0]
    received = lax.all_to_all(send_buffer, "dev", split_axis=0, concat_axis=0, tiled=True)
    flat_in = received.reshape(-1, feat_width)
    gated = jnp.dot(flat_in, gate_mat, preferred_element_type=jnp.float32)
    upward = jnp.dot(flat_in, up_mat, preferred_element_type=jnp.float32)
    act_half = (jax.nn.silu(gated) * upward).astype(jnp.bfloat16)
    result = jnp.dot(act_half, down_mat, preferred_element_type=jnp.float32).astype(jnp.bfloat16)
    part_rows = result.reshape(received.shape[0], received.shape[1], feat_width)
    finished = lax.psum_scatter(
        part_rows.astype(jnp.float32).astype(jnp.bfloat16), "grp", scatter_dimension=1, tiled=True
    )
    norm = gate_weight / jnp.sum(gate_weight, axis=1, keepdims=True)
    all_slots = lax.all_gather(finished, "grp", axis=1, tiled=True)
    returned = lax.all_to_all(all_slots, "dev", split_axis=0, concat_axis=0, tiled=True)
    picked = returned.reshape(-1, feat_width)[slot_index].reshape(tok_rows, top_count, feat_width)
    weighted = jnp.sum(picked.astype(jnp.float32) * norm[:, :, None], axis=1)
    return weighted.astype(jnp.bfloat16)


def solution(mesh):
    in_specs = (
        P("dev", None),
        P("dev", None),
        P("dev", None),
        P("dev", None, "grp"),
        P("dev", None, "grp"),
        P("dev", "grp", None),
    )
    out_specs = P("dev", None)
    return jax.shard_map(
        per_device, mesh=mesh, in_specs=in_specs, out_specs=out_specs, check_vma=False
    )
```

profile of v0, /device:TPU:82, one launch (start us, length us, event | category | flops | bytes accessed | tf_op | source)
XLA Modules:
  0.0 584.6 jit_solution(3882007921659991942)
XLA Ops:
  6.5 0.0 reduce-scatter.2.cloned.1.call-start
  6.5 0.8 copy.23
  7.3 0.1 eq.29
  7.4 0.1 eq.25
  7.5 0.7 broadcast_multiply_fusion
  8.2 18.0 %reduce-window.6 = s32[64,8,128]{2,1,0:T(8,128)S(1)} reduce-window(s32[64,8,128]{2,1,0:T(8,128)S(1)} %fusion.10, s32[]{:T(128)} %constant.33.clone.1), window={size=1x1x128 pad=0_0x0_0x127_0}, to_apply=%region_0.0 | reduce-window | flops 8323072 | bytes 524292 | tf_op jit(solution)/shard_map/reduce-window
  26.2 0.1 slice.12
  26.4 0.1 copy.25
  26.6 0.1 copy.26
  26.6 0.1 add_add_fusion
  26.8 0.1 copy.22
  26.9 0.1 mul.36
  27.0 0.1 fusion.9
  27.1 4.3 scatter_custom_fusion
  31.4 1.3 concatenate.3
  32.8 9.5 %gather_fusion = bf16[1536,4096]{1,0:T(8,128)(2,1)} fusion(bf16[129,4096]{1,0:T(8,128)(2,1)S(1)} %concatenate.3, s32[2048]{0:T(1024)S(1)} %pad_clamp_fusion), kind=kCustom, calls=%fused_computation | custom fusion | bytes 25171968 | tf_op jit(solution)/shard_map/gather | solution.py:22
  42.3 0.0 slice-start
  42.3 151.6 %all_to_all.10 = bf16[64,24,4096]{2,1,0:T(8,128)(2,1)S(1)} all-to-all(bf16[64,24,4096]{2,1,0:T(8,128)(2,1)} %bitcast.37), channel_id=1, replica_groups=mesh['grp'=2,'dev'=64] {'dev'}, dimensions={0} | all-to-all | bytes 25165824 | tf_op jit(solution)/shard_map/all_to_all | solution.py:26
  193.9 0.0 slice-start.1
  193.9 13.3 %fusion.2 = f32[1536,768]{1,0:T(8,128)} fusion(bf16[1536,4096]{1,0:T(8,128)(2,1)S(1)} %bitcast.38, bf16[1,4096,768]{2,1,0:T(8,128)(2,1)} %param.10), kind=kOutput, calls=%fused_computation.7 | convolution fusion | flops 9663676416 | bytes 23592960 | tf_op jit(solution)/shard_map/dot_general | solution.py:29
  207.2 0.0 slice-done
  207.2 0.0 slice-done.1
  207.2 12.2 %multiply_convert_fusion = bf16[1536,768]{1,0:T(8,128)(2,1)S(1)} fusion(f32[1536,768]{1,0:T(8,128)} %fusion.2, bf16[1536,4096]{1,0:T(8,128)(2,1)S(1)} %bitcast.39, bf16[1,4096,768]{2,1,0:T(8,128)(2,1)S(1)} %bitcast.47), kind=kOutput, calls=%fused_computation.11 | convolution fusion | flops 9670754304 | bytes 25952256 | tf_op jit(solution)/shard_map/dot_general | solution.py:28
  219.4 13.3 %convolution_convert_fusion = bf16[1536,4096]{1,0:T(8,128)(2,1)S(1)} fusion(bf16[1536,768]{1,0:T(8,128)(2,1)S(1)} %multiply_convert_fusion, bf16[1,768,4096]{2,1,0:T(8,128)(2,1)} %param.11), kind=kOutput, calls=%fused_computation.5 | convolution fusion | flops 9669967872 | bytes 21233664 | tf_op jit(solution)/shard_map/dot_general | solution.py:31
  232.7 16.4 %copy.27 = bf16[64,24,4096]{2,0,1:T(8,128)(2,1)} copy(bf16[64,24,4096]{2,1,0:T(8,128)(2,1)S(1)} %bitcast.40) | data formatting | bytes 25165824 | tf_op jit(solution)/shard_map/reshape | solution.py:32
  249.0 0.0 reduce-scatter.2.cloned.1.call-update
  249.1 0.0 all-gather.2.cloned.1.call-start
  249.1 26.1 %reduce-scatter.2.cloned.1.call-done = bf16[64,12,4096]{2,0,1:T(8,128)(2,1)} async-done(((bf16[64,24,4096]{2,0,1:T(8,128)(2,1)}), bf16[64,12,4096]{2,0,1:T(8,128)(2,1)}) %reduce-scatter.2.cloned.1.call-update) | async-done | bytes 6291472 | tf_op jit(solution)/shard_map/reduce_scatter | solution.py:33
  275.2 0.0 all-gather.2.cloned.1.call-update
  275.2 30.6 %all-gather.2.cloned.1.call-done = bf16[64,24,4096]{2,0,1:T(8,128)(2,1)} async-done(((bf16[64,12,4096]{2,0,1:T(8,128)(2,1)}), bf16[64,24,4096]{2,0,1:T(8,128)(2,1)}) %all-gather.2.cloned.1.call-update) | async-done | bytes 12582928 | tf_op jit(solution)/shard_map/all_gather | solution.py:37
  305.8 14.4 %copy.28 = bf16[64,24,4096]{2,1,0:T(8,128)(2,1)} copy(bf16[64,24,4096]{2,0,1:T(8,128)(2,1)} %all-gather.2.cloned.1.call-done) | data formatting | bytes 25165824 | tf_op jit(solution)/shard_map/all_gather | solution.py:37
  320.3 0.0 copy-start
  320.3 10.5 %all-to-all-start.1 = ((bf16[64,24,4096]{2,1,0:T(8,128)(2,1)}), bf16[64,24,4096]{2,1,0:T(8,128)(2,1)}, u32[]{:S(2)}, u32[]{:S(2)}) async-start(bf16[64,24,4096]{2,1,0:T(8,128)(2,1)} %copy.28), calls=%async_computation.2 | async-start | bytes 25165824 | tf_op jit(solution)/shard_map/all_to_all | solution.py:38
  330.8 0.0 copy-done
  330.9 0.1 copy.29
  331.0 212.6 %all-to-all-done.1 = bf16[64,24,4096]{2,1,0:T(8,128)(2,1)} async-done(((bf16[64,24,4096]{2,1,0:T(8,128)(2,1)}), bf16[64,24,4096]{2,1,0:T(8,128)(2,1)}, u32[]{:S(2)}, u32[]{:S(2)}) %all-to-all-start.1) | async-done | bytes 12582944 | tf_op jit(solution)/shard_map/all_to_all | solution.py:38
  543.6 21.3 %gather_fusion.1 = bf16[1024,4096]{1,0:T(8,128)(2,1)} fusion(bf16[1536,4096]{1,0:T(8,128)(2,1)} %bitcast.10, s32[1024]{0:T(1024)S(1)} %broadcast_clamp_fusion), kind=kCustom, calls=%fused_computation.1 | custom fusion | bytes 16781312 | tf_op jit(solution)/shard_map/gather | solution.py:39
  564.8 12.9 %fusion = bf16[128,4096]{1,0:T(8,128)(2,1)} fusion(bf16[1024,4096]{1,0:T(8,128)(2,1)} %gather_fusion.1, f32[128,8]{1,0:T(8,128)S(1)} %copy.29), kind=kLoop, calls=%fused_computation.4 | loop fusion | flops 12058624 | bytes 9441280 | tf_op jit(solution)/shard_map/reduce_sum | solution.py:40
  (11 shorter events, 0.1 us)
Async XLA Ops:
  6.5 268.7 %reduce-scatter.2.cloned.1.call-start = ((), (), s32[]{:S(2)}) async-start(), calls=%async_computation.3 | async-start | bytes 18874368 | tf_op jit(solution)/shard_map/reduce_scatter | solution.py:33
  42.3 164.9 %slice-start = ((s8[6291456]{0:T(1024)(128)(4,1)}), s8[4194304]{0:T(1024)(128)(4,1)S(1)}, s32[]{:S(2)}) async-start(s8[6291456]{0:T(1024)(128)(4,1)} %bitcast.46), calls=%async_computation.5 | async-start | bytes 8388608
  193.9 13.3 %slice-start.1 = ((s8[6291456]{0:T(1024)(128)(4,1)}), s8[2097152]{0:T(1024)(128)(4,1)S(1)}, s32[]{:S(2)}) async-start(s8[6291456]{0:T(1024)(128)(4,1)} %bitcast.46), calls=%async_computation.6 | async-start | bytes 4194304
  249.1 56.8 %all-gather.2.cloned.1.call-start = ((), (), s32[]{:S(2)}) async-start(), calls=%async_computation.4 | async-start | bytes 18874368 | tf_op jit(solution)/shard_map/all_gather | solution.py:37
  320.3 10.6 %copy-start = (f32[128,8]{0,1:T(8,128)S(1)}, f32[128,8]{0,1:T(8,128)}, u32[]{:S(2)}) copy-start(f32[128,8]{0,1:T(8,128)} %param.8) | copy-start | bytes 12292
  320.3 223.3 %all-to-all-start.1 = ((bf16[64,24,4096]{2,1,0:T(8,128)(2,1)}), bf16[64,24,4096]{2,1,0:T(8,128)(2,1)}, u32[]{:S(2)}, u32[]{:S(2)}) async-start(bf16[64,24,4096]{2,1,0:T(8,128)(2,1)} %copy.28), calls=%async_computation.2 | async-start | bytes 25165824 | tf_op jit(solution)/shard_map/all_to_all | solution.py:38
Sparse Core Ops, SparseCore 0:
  249.2 25.9 reduce-scatter.1
  276.9 28.9 all-gather.1
where the time goes:
time: 585 us
  waiting for transfers between devices  269 us (46%)
  blocking collectives  152 us (26%)
  local copies, waits for them, and re-layouts  68.9 us (12%)
  matrix products  38.8 us (7%)
  other arithmetic  31.9 us (5%)
  between operations  13.5 us (2%)
  starting transfers between devices  10.6 us (2%)
    all_to_all x1, waiting for transfers between devices, per_device(): lax.all_to_all(all_slots, 'dev', split_axis=0, concat_axis=0, tiled=True)  213 us
    all_to_all x1, blocking collectives, per_device(): lax.all_to_all(send_buffer, 'dev', split_axis=0, concat_axis=0, tiled=True)  152 us
    all_gather x1, waiting for transfers between devices, per_device(): all_slots = lax.all_gather(finished, 'grp', axis=1, tiled=True)  30.6 us
    reduce_scatter x1, waiting for transfers between devices, per_device(): lax.psum_scatter(part_rows.astype(jnp.float32).astype(jnp.bfloat16), 'grp...  26.1 us
    gather x1, local copies, waits for them, and re-layouts, per_device(): returned.reshape(-1, feat_width)[slot_index]  21.3 us
    another operation x2, other arithmetic  18 us
    reshape x1, local copies, waits for them, and re-layouts, per_device(): part_rows = result.reshape(received.shape[0], received.shape[1], feat_width)  16.4 us
    all_gather x1, local copies, waits for them, and re-layouts, per_device(): all_slots = lax.all_gather(finished, 'grp', axis=1, tiled=True)  14.4 us
  transfers between devices with their start and end apart: 3, of which 3 were waited for; matrix products, arithmetic and copies ran while one was open for 0% of the time, Pallas kernels for 0%

commit v1 on v0

v1 whole, which is shorter than its diff:
```python
import jax
import jax.numpy as jnp
from jax import lax
from jax.experimental import pallas as pl
from jax.experimental.pallas import tpu as pltpu
from jax.sharding import PartitionSpec as P

LARGE, SMALL = 8, 4
SWAP = ((0, 1), (1, 0))
VMEM = 48 * 2**20
COST = pl.CostEstimate(flops=1000, bytes_accessed=1000, transcendentals=0)


def dot(a, b):
    return jnp.dot(a, b, preferred_element_type=jnp.float32)


def hidden_kernel(x, gate, up, out):
    gated = dot(x[...], gate[0])
    upward = dot(x[...], up[0])
    out[...] = (jax.nn.silu(gated) * upward).astype(out.dtype)


def hidden_units(x, w_gate, w_up):
    m, width = x.shape
    ff = w_gate.shape[2]
    block = 256
    w_spec = pl.BlockSpec((1, width, block), lambda n: (0, 0, n))
    return pl.pallas_call(
        hidden_kernel,
        out_shape=jax.ShapeDtypeStruct((m, ff), jnp.bfloat16),
        grid=(ff // block,),
        in_specs=[pl.BlockSpec((m, width), lambda n: (0, 0)), w_spec, w_spec],
        out_specs=pl.BlockSpec((m, block), lambda n: (0, n)),
        compiler_params=pltpu.CompilerParams(vmem_limit_bytes=VMEM),
        cost_estimate=COST,
        name="hidden",
    )(x, w_gate, w_up)


def down_kernel(act_a, act_b, w_a, w_b, out):
    out[...] = (dot(act_a[...], w_a[0]) + dot(act_b[...], w_b[0])).astype(out.dtype)


def down(act_a, act_b, w_a, w_b):
    m, ff = act_a.shape
    width = w_a.shape[2]
    block = 512
    act_spec = pl.BlockSpec((m, ff), lambda n: (0, 0))
    w_spec = pl.BlockSpec((1, ff, block), lambda n: (0, 0, n))
    return pl.pallas_call(
        down_kernel,
        out_shape=jax.ShapeDtypeStruct((m, width), jnp.bfloat16),
        grid=(width // block,),
        in_specs=[act_spec, act_spec, w_spec, w_spec],
        out_specs=pl.BlockSpec((m, block), lambda n: (0, n)),
        compiler_params=pltpu.CompilerParams(vmem_limit_bytes=VMEM),
        cost_estimate=COST,
        name="down",
    )(act_a, act_b, w_a, w_b)


def exchange(a):
    return lax.all_to_all(a, "dev", split_axis=0, concat_axis=0, tiled=True)


def per_device(tokens, experts, gate_weight, w_gate, w_up, w_down):
    rows, width = tokens.shape
    n = lax.axis_size("dev")
    half = width // 2
    grp = lax.axis_index("grp").astype(jnp.int32)

    hit = experts[:, :, None] == jnp.arange(n, dtype=jnp.int32)[None, None, :]
    chosen = jnp.any(hit, axis=1)
    below = jnp.tril(jnp.ones((rows, rows), jnp.bfloat16), -1)
    earlier = dot(below, chosen.astype(jnp.bfloat16))
    rank = jnp.where(chosen, earlier.astype(jnp.int32), -1)
    norm = gate_weight / jnp.sum(gate_weight, axis=1, keepdims=True)
    weight = jnp.sum(jnp.where(hit, norm[:, :, None], 0.0), axis=1)
    rank_e = rank.T

    slots_0 = LARGE * grp + jnp.arange(LARGE, dtype=jnp.int32)
    slots_1 = 2 * LARGE + SMALL * grp + jnp.arange(SMALL, dtype=jnp.int32)
    sides = jnp.arange(2, dtype=jnp.int32)
    slots_1 = jnp.broadcast_to(slots_1[None, :], (2, SMALL)).reshape(-1)
    side_1 = jnp.broadcast_to(sides[:, None], (2, SMALL)).reshape(-1)

    pick_0 = (rank_e[:, None, :] == slots_0[None, :, None]).astype(jnp.bfloat16)
    send_0 = dot(pick_0.reshape(n * LARGE, rows), tokens).astype(jnp.bfloat16)
    same_side = side_1[None, :, None, None] == sides[None, None, :, None]
    pick_1 = (
        (rank_e[:, None, None, :] == slots_1[None, :, None, None]) & same_side
    ).astype(jnp.bfloat16)
    stacked = jnp.concatenate([tokens[:, :half], tokens[:, half:]], axis=0)
    send_1 = dot(pick_1.reshape(n * 2 * SMALL, 2 * rows), stacked).astype(jnp.bfloat16)

    m_1 = n * 2 * SMALL
    at = jnp.arange(m_1, dtype=jnp.int32)
    source = (at % (m_1 // 2)) // SMALL * (2 * SMALL) + at // (m_1 // 2) * SMALL + at % SMALL
    order = (source[:, None] == at[None, :]).astype(jnp.bfloat16)

    gate_b = lax.ppermute(w_gate, "grp", SWAP)
    up_b = lax.ppermute(w_up, "grp", SWAP)
    down_b = lax.ppermute(w_down, "grp", SWAP)

    def expert(x):
        act_a = hidden_units(x, w_gate, w_up)
        act_b = hidden_units(x, gate_b, up_b)
        return down(act_a, act_b, w_down, down_b)

    x_1 = exchange(send_1.reshape(n, 2 * SMALL, half))
    x_0 = exchange(send_0.reshape(n, LARGE, width))
    x_1 = dot(order, x_1.reshape(m_1, half)).astype(jnp.bfloat16)
    done_1 = expert(jnp.concatenate([x_1[: m_1 // 2], x_1[m_1 // 2 :]], axis=1))
    done_1 = jnp.concatenate([done_1[:, :half], done_1[:, half:]], axis=0)
    done_1 = dot(order.T, done_1).astype(jnp.bfloat16).reshape(n, 2 * SMALL, half)
    x_0, done_1 = lax.optimization_barrier((x_0, done_1))
    back_1 = exchange(done_1)
    done_0 = expert(x_0.reshape(n * LARGE, width)).reshape(n, LARGE, width)
    back_1, done_0 = lax.optimization_barrier((back_1, done_0))
    back_0 = exchange(done_0)

    high = lax.reduce_precision(weight, 8, 7)
    both = jnp.stack([high, weight - high]).astype(jnp.bfloat16)
    zero = jnp.bfloat16(0)
    here = (rank[None, None, :, :, None] == slots_1) & (sides[None, :, None, None, None] == side_1)
    place_1 = jnp.where(here, both[:, None, :, :, None], zero)
    total_1 = dot(place_1.reshape(4 * rows, m_1), back_1.reshape(m_1, half))
    total_1 = (total_1[: 2 * rows] + total_1[2 * rows :]).reshape(2, rows, half)
    total_1 = jnp.concatenate([total_1[0], total_1[1]], axis=1)
    place_0 = jnp.where(
        rank[None, :, :, None] == slots_0[None, None, None, :], both[:, :, :, None], zero
    ).reshape(2 * rows, n * LARGE)
    back_0, total_1, place_0 = lax.optimization_barrier((back_0, total_1, place_0))
    total_0 = dot(place_0, back_0.reshape(n * LARGE, width))
    part = (total_0[:rows] + total_0[rows:] + total_1).astype(jnp.bfloat16)
    theirs = lax.ppermute(part, "grp", SWAP)
    return (part.astype(jnp.float32) + theirs.astype(jnp.float32)).astype(jnp.bfloat16)


def solution(mesh):
    in_specs = (
        P("dev", None),
        P("dev", None),
        P("dev", None),
        P("dev", None, "grp"),
        P("dev", None, "grp"),
        P("dev", "grp", None),
    )
    return jax.shard_map(
        per_device, mesh=mesh, in_specs=in_specs, out_specs=P("dev", None), check_vma=False
    )
```

time: 585 us -> 223 us (0.38)
  the two profiles are of different devices: /device:TPU:82 before, /device:TPU:1 now
where the time goes in v1:
time: 223 us; the launch traced here: 220 us
  waiting for transfers between devices  94 us (42%)
  Pallas kernels  54.9 us (25%)
  starting transfers between devices  47.3 us (21%)
  matrix products  14.4 us (6%)
  other arithmetic  4.85 us (2%)
  local copies, waits for them, and re-layouts  4.17 us (2%)
    all_to_all x4, waiting for transfers between devices, exchange(): return lax.all_to_all(a, 'dev', split_axis=0, concat_axis=0, tiled=True)  91.7 us
    all_to_all x4, starting transfers between devices, exchange(): return lax.all_to_all(a, 'dev', split_axis=0, concat_axis=0, tiled=True)  40.6 us
    pallas_call x4, Pallas kernels, hidden_units(): pl.pallas_call(hidden_kernel, out_shape=jax.ShapeDtypeStruct((m, ff), jnp...  35.3 us
    pallas_call x2, Pallas kernels, down(): pl.pallas_call(down_kernel, out_shape=jax.ShapeDtypeStruct((m, width), jn...  19.6 us
    dot_general x7, matrix products, dot(): return jnp.dot(a, b, preferred_element_type=jnp.float32)  14.4 us
    ppermute x1, starting transfers between devices, per_device(): theirs = lax.ppermute(part, 'grp', SWAP)  4.77 us
  transfers between devices with their start and end apart: 8, of which 4 were waited for; matrix products, arithmetic and copies ran while one was open for 7% of the time, Pallas kernels for 25%

profile of v1, /device:TPU:1, one launch (start us, length us, event | category | flops | bytes accessed | tf_op | source)
XLA Modules:
  0.0 220.0 jit_solution(2606612175498944304)
XLA Ops:
  0.0 1.4 collective-permute-start
  1.4 0.0 collective-permute-start.1
  1.4 0.5 collective-permute-start.2
  1.9 0.7 fusion.22
  2.7 0.1 eq.159
  2.8 0.2 fusion.13
  3.0 0.1 broadcast_compare_fusion.2
  3.1 0.1 eq.162
  3.2 1.3 fusion.58
  4.5 2.1 fusion.3
  6.5 11.3 %all-to-all-start.1 = ((bf16[64,8,2048]{2,1,0:T(8,128)(2,1)}), bf16[64,8,2048]{2,1,0:T(8,128)(2,1)S(1)}, u32[]{:S(2)}, u32[]{:S(2)}) async-start(bf16[64,8,2048]{2,1,0:T(8,128)(2,1)} %fusion.3), calls=%async_computation.1 | async-start | bytes 4194304 | tf_op jit(solution)/shard_map/all_to_all | solution.py:64
  17.9 0.1 eq.153
  18.0 3.3 %fusion = bf16[64,8,4096]{2,1,0:T(8,128)(2,1)} fusion(bf16[128,4096]{1,0:T(8,128)(2,1)S(1)} %copy-done.1, s32[512]{0:T(512)S(1)} %eq.153, s32[64,128]{1,0:T(8,128)S(1)} %bitcast.44), kind=kOutput, calls=%fused_computation.1 | convolution fusion | flops 539033600 | bytes 5277696 | tf_op jit(solution)/shard_map/dot_general | solution.py:15
  21.3 25.0 %all-to-all-done.1 = bf16[64,8,2048]{2,1,0:T(8,128)(2,1)S(1)} async-done(((bf16[64,8,2048]{2,1,0:T(8,128)(2,1)}), bf16[64,8,2048]{2,1,0:T(8,128)(2,1)S(1)}, u32[]{:S(2)}, u32[]{:S(2)}) %all-to-all-start.1) | async-done | bytes 2097184 | tf_op jit(solution)/shard_map/all_to_all | solution.py:64
  46.3 7.1 %all-to-all-start = ((bf16[64,8,4096]{2,1,0:T(8,128)(2,1)}), bf16[64,8,4096]{2,1,0:T(8,128)(2,1)}, u32[]{:S(2)}, u32[]{:S(2)}) async-start(bf16[64,8,4096]{2,1,0:T(8,128)(2,1)} %fusion), calls=%async_computation | async-start | bytes 8388608 | tf_op jit(solution)/shard_map/all_to_all | solution.py:64
  53.4 1.3 convolution_convert_fusion.3
  54.7 0.1 fusion.57
  54.8 0.2 pad_maximum_fusion.x
  55.1 7.0 %hidden.4.act_a = bf16[256,768]{1,0:T(8,128)(2,1)S(1)} custom-call(bf16[256,4096]{1,0:T(8,128)(2,1)S(1)} %pad_maximum_fusion.x, bf16[1,4096,768]{2,1,0:T(8,128)(2,1)} %gate.3, bf16[1,4096,768]{2,1,0:T(8,128)(2,1)} %up.3), custom_call_target="tpu_custom_call" | custom-call | flops 1000 | bytes 1000 | tf_op jit(solution)/shard_map/hidden/pallas_call | solution.py:29
  62.1 0.0 collective-permute-done.gate
  62.1 7.1 %hidden.5.act_b = bf16[256,768]{1,0:T(8,128)(2,1)S(1)} custom-call(bf16[256,4096]{1,0:T(8,128)(2,1)S(1)} %pad_maximum_fusion.x, bf16[1,4096,768]{2,1,0:T(8,128)(2,1)} %collective-permute-done.gate, bf16[1,4096,768]{2,1,0:T(8,128)(2,1)} %collective-permute-done.1.up), custom_call_target="tpu_custom_call" | custom-call | flops 1000 | bytes 1000 | tf_op jit(solution)/shard_map/hidden/pallas_call | solution.py:29
  69.2 0.0 collective-permute-done.2.w_b
  69.3 8.8 %down.2 = bf16[256,4096]{1,0:T(8,128)(2,1)S(1)} custom-call(bf16[256,768]{1,0:T(8,128)(2,1)S(1)} %hidden.4.act_a, bf16[256,768]{1,0:T(8,128)(2,1)S(1)} %hidden.5.act_b, bf16[1,768,4096]{2,1,0:T(8,128)(2,1)} %w_a.3, bf16[1,768,4096]{2,1,0:T(8,128)(2,1)} %collective-permute-done.2.w_b), custom_call_target="tpu_custom_call" | custom-call | flops 1000 | bytes 1000 | tf_op jit(solution)/shard_map/down/pallas_call | solution.py:51
  78.1 0.1 fusion.56
  78.2 2.7 %fusion.4 = bf16[64,8,2048]{2,1,0:T(8,128)(2,1)} fusion(bf16[256,2048]{1,0:T(8,128)(2,1)S(1)} %get-tuple-element.22, bf16[256,2048]{1,0:T(8,128)(2,1)S(1)} %get-tuple-element.21, s32[512]{0:T(512)S(1)} %fusion.44), kind=kOutput, calls=%fused_computation.8 | convolution fusion | flops 1079246848 | bytes 4196352 | tf_op jit(solution)/shard_map/dot_general | solution.py:15
  80.9 23.4 %all-to-all-done = bf16[64,8,4096]{2,1,0:T(8,128)(2,1)} async-done(((bf16[64,8,4096]{2,1,0:T(8,128)(2,1)}), bf16[64,8,4096]{2,1,0:T(8,128)(2,1)}, u32[]{:S(2)}, u32[]{:S(2)}) %all-to-all-start) | async-done | bytes 4194336 | tf_op jit(solution)/shard_map/all_to_all | solution.py:64
  104.3 12.2 %all-to-all-start.2 = ((bf16[64,8,2048]{2,1,0:T(8,128)(2,1)}), bf16[64,8,2048]{2,1,0:T(8,128)(2,1)S(1)}, u32[]{:S(2)}, u32[]{:S(2)}) async-start(bf16[64,8,2048]{2,1,0:T(8,128)(2,1)} %fusion.4), calls=%async_computation.2 | async-start | bytes 4194304 | tf_op jit(solution)/shard_map/all_to_all | solution.py:64
  116.5 10.6 %hidden.6.act_a = bf16[512,768]{1,0:T(8,128)(2,1)S(1)} custom-call(bf16[512,4096]{1,0:T(8,128)(2,1)} %bitcast.7.x, bf16[1,4096,768]{2,1,0:T(8,128)(2,1)} %gate.3, bf16[1,4096,768]{2,1,0:T(8,128)(2,1)} %up.3), custom_call_target="tpu_custom_call" | custom-call | flops 1000 | bytes 1000 | tf_op jit(solution)/shard_map/hidden/pallas_call | solution.py:29
  127.1 10.6 %hidden.7.act_b = bf16[512,768]{1,0:T(8,128)(2,1)S(1)} custom-call(bf16[512,4096]{1,0:T(8,128)(2,1)} %bitcast.7.x, bf16[1,4096,768]{2,1,0:T(8,128)(2,1)} %collective-permute-done.gate, bf16[1,4096,768]{2,1,0:T(8,128)(2,1)} %collective-permute-done.1.up), custom_call_target="tpu_custom_call" | custom-call | flops 1000 | bytes 1000 | tf_op jit(solution)/shard_map/hidden/pallas_call | solution.py:29
  137.7 10.8 %down.3 = bf16[512,4096]{1,0:T(8,128)(2,1)S(1)} custom-call(bf16[512,768]{1,0:T(8,128)(2,1)S(1)} %hidden.6.act_a, bf16[512,768]{1,0:T(8,128)(2,1)S(1)} %hidden.7.act_b, bf16[1,768,4096]{2,1,0:T(8,128)(2,1)} %w_a.3, bf16[1,768,4096]{2,1,0:T(8,128)(2,1)} %collective-permute-done.2.w_b), custom_call_target="tpu_custom_call" | custom-call | flops 1000 | bytes 1000 | tf_op jit(solution)/shard_map/down/pallas_call | solution.py:51
  148.5 1.9 copy-done
  150.5 10.0 %all-to-all-start.3 = ((bf16[64,8,4096]{2,1,0:T(8,128)(2,1)}), bf16[64,8,4096]{2,1,0:T(8,128)(2,1)}, u32[]{:S(2)}, u32[]{:S(2)}) async-start(bf16[64,8,4096]{2,1,0:T(8,128)(2,1)} %bitcast.41), calls=%async_computation.3 | async-start | bytes 8388608 | tf_op jit(solution)/shard_map/all_to_all | solution.py:64
  160.7 0.1 iota_compare_fusion.5
  160.7 0.1 broadcast_compare_fusion
  160.9 0.4 broadcast_and_fusion
  161.2 0.6 broadcast_select_fusion
  161.9 0.2 select_n.90
  162.1 0.4 fusion.21
  162.6 1.3 fusion.10
  163.9 0.3 slice_add_fusion.1
  164.2 0.1 fusion.55
  164.4 0.1 pad_maximum_fusion.1
  164.5 43.4 %all-to-all-done.3 = bf16[64,8,4096]{2,1,0:T(8,128)(2,1)} async-done(((bf16[64,8,4096]{2,1,0:T(8,128)(2,1)}), bf16[64,8,4096]{2,1,0:T(8,128)(2,1)}, u32[]{:S(2)}, u32[]{:S(2)}) %all-to-all-start.3) | async-done | bytes 4194336 | tf_op jit(solution)/shard_map/all_to_all | solution.py:64
  207.9 3.5 %fusion.1 = f32[256,4096]{1,0:T(8,128)S(1)} fusion(bf16[256,512]{0,1:T(8,128)(2,1)S(1)} %bitcast.42, bf16[64,8,4096]{2,1,0:T(8,128)(2,1)} %all-to-all-done.3), kind=kOutput, calls=%fused_computation.2 | convolution fusion | flops 1073741824 | bytes 8650752 | tf_op jit(solution)/shard_map/dot_general | solution.py:15
  211.4 0.3 fusion.6
  211.7 4.8 %collective-permute-start.3 = (bf16[128,4096]{1,0:T(8,128)(2,1)S(1)}, bf16[128,4096]{1,0:T(8,128)(2,1)S(1)}, u32[]{:S(2)}, u32[]{:S(2)}) collective-permute-start(bf16[128,4096]{1,0:T(8,128)(2,1)S(1)} %fusion.6), channel_id=1, source_target_pairs={{0,64},{64,0},{1,65},{65,1},{2,66},{66,2},{3,67},{67,3},{4,68},{68... | collective-permute-start | bytes 3145736 | tf_op jit(solution)/shard_map/ppermute | solution.py:137
  216.5 2.3 %collective-permute-done.3 = bf16[128,4096]{1,0:T(8,128)(2,1)S(1)} collective-permute-done((bf16[128,4096]{1,0:T(8,128)(2,1)S(1)}, bf16[128,4096]{1,0:T(8,128)(2,1)S(1)}, u32[]{:S(2)}, u32[]{:S(2)}) %collective-permute-start.3) | collective-permute-done | bytes 1048608 | tf_op jit(solution)/shard_map/ppermute | solution.py:137
  218.8 1.2 add_convert_fusion
  (24 shorter events, 0.2 us)
Async XLA Ops:
  0.0 62.1 %collective-permute-start = (bf16[1,4096,768]{2,1,0:T(8,128)(2,1)}, bf16[1,4096,768]{2,1,0:T(8,128)(2,1)}, u32[]{:S(2)}, u32[]{:S(2)}) collective-permute-start(bf16[1,4096,768]{2,1,0:T(8,128)(2,1)} %gate.3), channel_id=1, source_target_pairs={{0,64},{64,0},{1,65},{65,1},{2,66},{66,2},{3,67},{67,3},{4,68},{68... | collective-permute-start | bytes 18874376 | tf_op jit(solution)/shard_map/ppermute | solution.py:102
  1.4 60.7 %collective-permute-start.1 = (bf16[1,4096,768]{2,1,0:T(8,128)(2,1)}, bf16[1,4096,768]{2,1,0:T(8,128)(2,1)}, u32[]{:S(2)}, u32[]{:S(2)}) collective-permute-start(bf16[1,4096,768]{2,1,0:T(8,128)(2,1)} %up.3), channel_id=1, source_target_pairs={{0,64},{64,0},{1,65},{65,1},{2,66},{66,2},{3,67},{67,3},{4,68},{68... | collective-permute-start | bytes 18874376 | tf_op jit(solution)/shard_map/ppermute | solution.py:103
  1.4 67.8 %collective-permute-start.2 = (bf16[1,768,4096]{2,1,0:T(8,128)(2,1)}, bf16[1,768,4096]{2,1,0:T(8,128)(2,1)}, u32[]{:S(2)}, u32[]{:S(2)}) collective-permute-start(bf16[1,768,4096]{2,1,0:T(8,128)(2,1)} %w_a.3), channel_id=1, source_target_pairs={{0,64},{64,0},{1,65},{65,1},{2,66},{66,2},{3,67},{67,3},{4,68},{68... | collective-permute-start | bytes 18874376 | tf_op jit(solution)/shard_map/ppermute | solution.py:104
  6.5 11.5 %copy-start.1 = (bf16[128,4096]{1,0:T(8,128)(2,1)S(1)}, bf16[128,4096]{1,0:T(8,128)(2,1)}, u32[]{:S(2)}) copy-start(bf16[128,4096]{1,0:T(8,128)(2,1)} %param.6) | copy-start | bytes 3145732
  6.5 39.8 %all-to-all-start.1 = ((bf16[64,8,2048]{2,1,0:T(8,128)(2,1)}), bf16[64,8,2048]{2,1,0:T(8,128)(2,1)S(1)}, u32[]{:S(2)}, u32[]{:S(2)}) async-start(bf16[64,8,2048]{2,1,0:T(8,128)(2,1)} %fusion.3), calls=%async_computation.1 | async-start | bytes 4194304 | tf_op jit(solution)/shard_map/all_to_all | solution.py:64
  46.3 58.0 %all-to-all-start = ((bf16[64,8,4096]{2,1,0:T(8,128)(2,1)}), bf16[64,8,4096]{2,1,0:T(8,128)(2,1)}, u32[]{:S(2)}, u32[]{:S(2)}) async-start(bf16[64,8,4096]{2,1,0:T(8,128)(2,1)} %fusion), calls=%async_computation | async-start | bytes 8388608 | tf_op jit(solution)/shard_map/all_to_all | solution.py:64
  104.3 46.2 %all-to-all-start.2 = ((bf16[64,8,2048]{2,1,0:T(8,128)(2,1)}), bf16[64,8,2048]{2,1,0:T(8,128)(2,1)S(1)}, u32[]{:S(2)}, u32[]{:S(2)}) async-start(bf16[64,8,2048]{2,1,0:T(8,128)(2,1)} %fusion.4), calls=%async_computation.2 | async-start | bytes 4194304 | tf_op jit(solution)/shard_map/all_to_all | solution.py:64
  148.5 1.9 copy-start
  150.5 10.0 %copy-start.3 = (f32[128,8]{0,1:T(8,128)S(1)}, f32[128,8]{0,1:T(8,128)}, u32[]{:S(2)}) copy-start(f32[128,8]{0,1:T(8,128)} %param.8) | copy-start | bytes 12292
  150.5 10.1 %copy-start.2 = (s32[128,8]{0,1:T(8,128)S(1)}, s32[128,8]{0,1:T(8,128)}, u32[]{:S(2)}) copy-start(s32[128,8]{0,1:T(8,128)} %param.7) | copy-start | bytes 12292
  150.5 57.4 %all-to-all-start.3 = ((bf16[64,8,4096]{2,1,0:T(8,128)(2,1)}), bf16[64,8,4096]{2,1,0:T(8,128)(2,1)}, u32[]{:S(2)}, u32[]{:S(2)}) async-start(bf16[64,8,4096]{2,1,0:T(8,128)(2,1)} %bitcast.41), calls=%async_computation.3 | async-start | bytes 8388608 | tf_op jit(solution)/shard_map/all_to_all | solution.py:64
  211.7 7.1 %collective-permute-start.3 = (bf16[128,4096]{1,0:T(8,128)(2,1)S(1)}, bf16[128,4096]{1,0:T(8,128)(2,1)S(1)}, u32[]{:S(2)}, u32[]{:S(2)}) collective-permute-start(bf16[128,4096]{1,0:T(8,128)(2,1)S(1)} %fusion.6), channel_id=1, source_target_pairs={{0,64},{64,0},{1,65},{65,1},{2,66},{66,2},{3,67},{67,3},{4,68},{68... | collective-permute-start | bytes 3145736 | tf_op jit(solution)/shard_map/ppermute | solution.py:137

commit v2 on v1

v2 whole, which is shorter than its diff:
```python
import jax
import jax.numpy as jnp
from jax import lax
from jax.experimental import pallas as pl
from jax.experimental.pallas import tpu as pltpu
from jax.sharding import PartitionSpec as P

SLOTS, QUARTERS = 6, 4
GROUP = 16
SWAP = ((0, 1), (1, 0))
VMEM = 48 * 2**20
COST = pl.CostEstimate(flops=1000, bytes_accessed=1000, transcendentals=0)


def dot(a, b):
    return jnp.dot(a, b, preferred_element_type=jnp.float32)


def order_rows(order, x, rows):
    size = order.shape[0]
    quarter = x.shape[1]
    count = size // QUARTERS
    for g in range(x.shape[0] // size):
        y = dot(order[...], x[g * size : (g + 1) * size]).astype(rows.dtype)
        for q in range(QUARTERS):
            rows[g * count : (g + 1) * count, q * quarter : (q + 1) * quarter] = y[
                q * count : (q + 1) * count
            ]


def hidden_kernel(x, gate, up, out):
    gated = dot(x[...], gate[0])
    upward = dot(x[...], up[0])
    out[...] = (jax.nn.silu(gated) * upward).astype(out.dtype)


def first_hidden_kernel(order, x, gate, up, out, rows):
    @pl.when(pl.program_id(0) == 0)
    def _():
        order_rows(order, x, rows)

    hidden_kernel(rows, gate, up, out)


def whole(shape):
    return pl.BlockSpec(shape, lambda i: (0,) * len(shape))


def params():
    return dict(
        compiler_params=pltpu.CompilerParams(vmem_limit_bytes=VMEM), cost_estimate=COST
    )


def hidden_units(x, w_gate, w_up, order=None):
    ff = w_gate.shape[2]
    width = w_gate.shape[1]
    m = x.size // width
    block = 256
    w_spec = pl.BlockSpec((1, width, block), lambda n: (0, 0, n))
    act = jax.ShapeDtypeStruct((m, ff), jnp.bfloat16)
    act_spec = pl.BlockSpec((m, block), lambda n: (0, n))
    if order is None:
        return pl.pallas_call(
            hidden_kernel,
            out_shape=act,
            grid=(ff // block,),
            in_specs=[whole(x.shape), w_spec, w_spec],
            out_specs=act_spec,
            name="hidden",
            **params(),
        )(x, w_gate, w_up)
    return pl.pallas_call(
        first_hidden_kernel,
        out_shape=[act, jax.ShapeDtypeStruct((m, width), x.dtype)],
        grid=(ff // block,),
        in_specs=[whole(order.shape), whole(x.shape), w_spec, w_spec],
        out_specs=[act_spec, whole((m, width))],
        name="first_hidden",
        **params(),
    )(order, x, w_gate, w_up)


def down_kernel(order_t, act_a, act_b, w_a, w_b, out, rows):
    step = pl.program_id(0)
    width = rows.shape[1]
    block = w_a.shape[2]
    steps = width // block
    size, quarter = out.shape
    count = size // QUARTERS

    @pl.when(step < steps)
    def _():
        part = dot(act_a[...], w_a[0]) + dot(act_b[...], w_b[0])
        rows[:, pl.ds(pl.multiple_of(step * block, block), block)] = part.astype(rows.dtype)

    @pl.when(step >= steps)
    def _():
        here = pl.ds(pl.multiple_of((step - steps) * count, count), count)
        parts = [rows[here, q * quarter : (q + 1) * quarter] for q in range(QUARTERS)]
        out[...] = dot(order_t[...], jnp.concatenate(parts, axis=0)).astype(out.dtype)


def down(order_t, act_a, act_b, w_a, w_b):
    m, ff = act_a.shape
    width = w_a.shape[2]
    block = 512
    steps = width // block
    size = order_t.shape[0]
    quarter = width // QUARTERS
    w_spec = pl.BlockSpec((1, ff, block), lambda i: (0, 0, jnp.minimum(i, steps - 1)))
    return pl.pallas_call(
        down_kernel,
        out_shape=jax.ShapeDtypeStruct((m * QUARTERS, quarter), jnp.bfloat16),
        grid=(steps + m * QUARTERS // size,),
        in_specs=[whole(order_t.shape), whole(act_a.shape), whole(act_b.shape), w_spec, w_spec],
        out_specs=pl.BlockSpec((size, quarter), lambda i: (jnp.maximum(i - steps, 0), 0)),
        scratch_shapes=[pltpu.VMEM((m, width), jnp.bfloat16)],
        name="down",
        **params(),
    )(order_t, act_a, act_b, w_a, w_b)


def pack_kernel(expand, row_slot, row_quarter, rank, tokens, out, stacked):
    quarter = out.shape[1]
    rows = tokens.shape[0]

    @pl.when(pl.program_id(0) == 0)
    def _():
        for q in range(QUARTERS):
            stacked[q * rows : (q + 1) * rows] = tokens[:, q * quarter : (q + 1) * quarter]

    found = dot(expand[...], rank[...]) == row_slot[...]
    picks = [
        jnp.where(found & (row_quarter[...] == q), 1.0, 0.0).astype(jnp.bfloat16)
        for q in range(QUARTERS)
    ]
    out[...] = dot(jnp.concatenate(picks, axis=1), stacked[...]).astype(out.dtype)


def pack(first, rank, tokens):
    n, rows = rank.shape
    quarter = tokens.shape[1] // QUARTERS
    step = 16
    part = SLOTS * QUARTERS
    at = jnp.arange(step * part, dtype=jnp.int32)
    wide = (step * part, rows)
    expand = (at[:, None] // part == jnp.arange(step)[None, :]).astype(jnp.bfloat16)
    row_slot = jnp.broadcast_to((first + at % SLOTS).astype(jnp.float32)[:, None], wide)
    row_quarter = jnp.broadcast_to((at % part // SLOTS).astype(jnp.float32)[:, None], wide)
    return pl.pallas_call(
        pack_kernel,
        out_shape=jax.ShapeDtypeStruct((n * part, quarter), jnp.bfloat16),
        grid=(n // step,),
        in_specs=[
            whole(expand.shape),
            whole(wide),
            whole(wide),
            pl.BlockSpec((step, rows), lambda i: (i, 0)),
            whole(tokens.shape),
        ],
        out_specs=pl.BlockSpec((step * part, quarter), lambda i: (i, 0)),
        scratch_shapes=[pltpu.VMEM((QUARTERS * rows, quarter), jnp.bfloat16)],
        name="pack",
        **params(),
    )(expand, row_slot, row_quarter, rank, tokens)


def combine_kernel(order, placed, back, before, out, lines):
    size, quarter = back.shape
    rows = out.shape[0]
    count = size // QUARTERS
    step = pl.program_id(0)
    y = dot(order[...], back[...]).astype(back.dtype)
    for q in range(QUARTERS):
        lines[
            pl.ds(pl.multiple_of(step * count, count), count), q * quarter : (q + 1) * quarter
        ] = y[q * count : (q + 1) * count]

    @pl.when(step == pl.num_programs(0) - 1)
    def _():
        for q in range(QUARTERS):
            here = slice(q * quarter, (q + 1) * quarter)
            both = dot(placed[...], lines[:, here])
            out[:, here] = (both[:rows] + both[rows:] + before[:, here]).astype(out.dtype)


def combine(order, placed, back, before, kind):
    size = order.shape[0]
    quarter = back.shape[1]
    return pl.pallas_call(
        combine_kernel,
        out_shape=jax.ShapeDtypeStruct(before.shape, kind),
        grid=(back.shape[0] // size,),
        in_specs=[
            whole(order.shape),
            whole(placed.shape),
            pl.BlockSpec((size, quarter), lambda i: (i, 0)),
            whole(before.shape),
        ],
        out_specs=whole(before.shape),
        scratch_shapes=[pltpu.VMEM((placed.shape[1], QUARTERS * quarter), back.dtype)],
        name="combine",
        **params(),
    )(order, placed, back, before)


def per_device(tokens, experts, gate_weight, w_gate, w_up, w_down):
    rows, width = tokens.shape
    n = lax.axis_size("dev")
    half = width // 2
    grp = lax.axis_index("grp").astype(jnp.int32)

    hit = experts[:, :, None] == jnp.arange(n, dtype=jnp.int32)[None, None, :]
    chosen = jnp.any(hit, axis=1)
    below = jnp.tril(jnp.ones((rows, rows), jnp.bfloat16), -1)
    earlier = dot(below, chosen.astype(jnp.bfloat16))
    rank = jnp.where(chosen, earlier.astype(jnp.int32), -1)
    norm = gate_weight / jnp.sum(gate_weight, axis=1, keepdims=True)
    weight = jnp.sum(jnp.where(hit, norm[:, :, None], 0.0), axis=1)
    rank_e = rank.T.astype(jnp.bfloat16)

    part = SLOTS * QUARTERS
    quarter = width // QUARTERS
    firsts = [(2 * grp + piece) * SLOTS for piece in range(2)]

    size = GROUP * part
    at = jnp.arange(size, dtype=jnp.int32)
    source = (at // SLOTS) % GROUP * part + at // (GROUP * SLOTS) * SLOTS + at % SLOTS
    order = (source[:, None] == at[None, :]).astype(jnp.bfloat16)
    order_t = (at[:, None] == source[None, :]).astype(jnp.bfloat16)

    gate_b = lax.ppermute(w_gate, "grp", SWAP)
    up_b = lax.ppermute(w_up, "grp", SWAP)
    down_b = lax.ppermute(w_down, "grp", SWAP)

    def expert(x):
        act_a, lines = hidden_units(x, w_gate, w_up, order)
        act_b = hidden_units(lines, gate_b, up_b)
        return down(order_t, act_a, act_b, w_down, down_b)

    def exchange(a):
        a = a.reshape(n, part, quarter)
        a = lax.all_to_all(a, "dev", split_axis=0, concat_axis=0, tiled=True)
        return a.reshape(n * part, quarter)

    x_0 = exchange(pack(firsts[0], rank_e, tokens))
    x_1 = exchange(pack(firsts[1], rank_e, tokens))
    done_0 = expert(x_0)
    x_1, done_0 = lax.optimization_barrier((x_1, done_0))
    back_0 = exchange(done_0)
    done_1 = expert(x_1)
    back_0, done_1 = lax.optimization_barrier((back_0, done_1))
    back_1 = exchange(done_1)

    high = lax.reduce_precision(weight, 8, 7)
    both = jnp.concatenate([high, weight - high], axis=0).astype(jnp.bfloat16)
    rank_2 = jnp.concatenate([rank, rank], axis=0)

    def place(piece):
        slots = firsts[piece] + jnp.arange(SLOTS, dtype=jnp.int32)
        at_row = jnp.where(rank_2[:, :, None] == slots, both[:, :, None], jnp.bfloat16(0))
        return at_row.reshape(2 * rows, n * SLOTS)

    nothing = jnp.zeros((rows, width), jnp.float32)
    total_0 = combine(order, place(0), back_0, nothing, jnp.float32)
    back_1, total_0, placed = lax.optimization_barrier((back_1, total_0, place(1)))
    mine = combine(order, placed, back_1, total_0, jnp.bfloat16)
    theirs = lax.ppermute(mine, "grp", SWAP)
    return (mine.astype(jnp.float32) + theirs.astype(jnp.float32)).astype(jnp.bfloat16)


def solution(mesh):
    in_specs = (
        P("dev", None),
        P("dev", None),
        P("dev", None),
        P("dev", None, "grp"),
        P("dev", None, "grp"),
        P("dev", "grp", None),
    )
    return jax.shard_map(
        per_device, mesh=mesh, in_specs=in_specs, out_specs=P("dev", None), check_vma=False
    )
```

time: 223 us -> 214 us (0.960); the launches traced: 220 us -> 213 us
  Pallas kernels: 54.9 us -> 83.9 us
  waiting for transfers between devices: 94 us -> 79 us
  matrix products: 14.4 us -> 0.2 us
  starting transfers between devices: 47.3 us -> 44.8 us
  other arithmetic: 4.85 us -> 2.55 us
    pallas_call x6 -> x10, Pallas kernels: 54.9 us -> 83.9 us  [the longest x2 27 us: down(): pl.pallas_call(down_kernel, out_shape=jax.ShapeDtypeStruct((m * QUARTERS,...]
    all_to_all x4, waiting for transfers between devices: 91.7 us -> 76.8 us  [exchange(): a = lax.all_to_all(a, 'dev', split_axis=0, concat_axis=0, tiled=True)]
    dot_general x7 -> x1, matrix products: 14.4 us -> 0.2 us  [dot(): return jnp.dot(a, b, preferred_element_type=jnp.float32)]
  transfers between devices with their start and end apart: 8 -> 8, of which waited for: 4 -> 5; matrix products, arithmetic and copies ran while one was open for 7% -> 1% of each run, Pallas kernels for 25% -> 37%
where the time goes in v2:
time: 214 us; the launch traced here: 213 us
  Pallas kernels  83.9 us (39%)
  waiting for transfers between devices  79 us (37%)
  starting transfers between devices  44.8 us (21%)
  other arithmetic  2.55 us (1%)
  local copies, waits for them, and re-layouts  2.55 us (1%)
    all_to_all x4, waiting for transfers between devices, exchange(): a = lax.all_to_all(a, 'dev', split_axis=0, concat_axis=0, tiled=True)  76.8 us
    all_to_all x4, starting transfers between devices, exchange(): a = lax.all_to_all(a, 'dev', split_axis=0, concat_axis=0, tiled=True)  39.9 us
    pallas_call x2, Pallas kernels, down(): pl.pallas_call(down_kernel, out_shape=jax.ShapeDtypeStruct((m * QUARTERS,...  27 us
    pallas_call x2, Pallas kernels, hidden_units(): pl.pallas_call(first_hidden_kernel, out_shape=[act, jax.ShapeDtypeStruct(...  21.8 us
    pallas_call x2, Pallas kernels, hidden_units(): pl.pallas_call(hidden_kernel, out_shape=act, grid=(ff // block,), in_spec...  16.6 us
    pallas_call x2, Pallas kernels, combine(): pl.pallas_call(combine_kernel, out_shape=jax.ShapeDtypeStruct(before.shap...  10.7 us
    pallas_call x2, Pallas kernels, pack(): pl.pallas_call(pack_kernel, out_shape=jax.ShapeDtypeStruct((n * part, qua...  7.83 us
  transfers between devices with their start and end apart: 8, of which 5 were waited for; matrix products, arithmetic and copies ran while one was open for 1% of the time, Pallas kernels for 37%

profile of v2, /device:TPU:1, one launch (start us, length us, event | category | flops | bytes accessed | tf_op | source)
XLA Modules:
  0.0 213.4 jit_solution(14173375798761144479)
XLA Ops:
  0.0 1.4 collective-permute-start
  1.4 0.0 collective-permute-start.1
  1.4 0.5 collective-permute-start.2
  2.0 0.1 fusion.4.expand
  2.1 0.7 fusion.3
  2.8 0.2 fusion
  3.1 0.1 broadcast_in_dim.47.row_quarter
  3.2 0.1 broadcast_in_dim.55.row_slot
  3.3 0.0 copy-start
  3.3 1.2 copy-done
  4.5 3.9 %pack.3 = bf16[1536,1024]{1,0:T(8,128)(2,1)} custom-call(bf16[384,16]{1,0:T(8,128)(2,1)S(1)} %fusion.4.expand, f32[384,128]{1,0:T(8,128)S(1)} %broadcast_in_dim.55.row_slot, f32[384,128]{1,0:T(8,128)S(1)} %broadcast_in_dim.47.row_quarter, bf16[64,128]{1,0:T(8,128)(2,1)S(1)} %convert_bitcast_fusion.rank, bf16[128,4096]{1,0:T(8,128)(2,1)S(1)} %copy-done), custom_call_target="tpu_custom_call" | custom-call | flops 1000 | bytes 1000 | tf_op jit(solution)/shard_map/pack/pallas_call | solution.py:151
  8.5 0.0 copy-start.1
  8.5 11.6 %all-to-all-start.1 = ((bf16[64,24,1024]{2,1,0:T(8,128)(2,1)}), bf16[64,24,1024]{2,1,0:T(8,128)(2,1)}, u32[]{:S(2)}, u32[]{:S(2)}) async-start(bf16[64,24,1024]{2,1,0:T(8,128)(2,1)} %bitcast.3), calls=%async_computation.1 | async-start | bytes 6291456 | tf_op jit(solution)/shard_map/all_to_all | solution.py:244
  20.1 0.1 broadcast_in_dim.46.row_slot
  20.2 0.0 copy-done.1
  20.2 3.9 %pack.2 = bf16[1536,1024]{1,0:T(8,128)(2,1)} custom-call(bf16[384,16]{1,0:T(8,128)(2,1)S(1)} %fusion.4.expand, f32[384,128]{1,0:T(8,128)S(1)} %broadcast_in_dim.46.row_slot, f32[384,128]{1,0:T(8,128)S(1)} %broadcast_in_dim.47.row_quarter, bf16[64,128]{1,0:T(8,128)(2,1)S(1)} %convert_bitcast_fusion.rank, bf16[128,4096]{1,0:T(8,128)(2,1)S(1)} %copy-done.1), custom_call_target="tpu_custom_call" | custom-call | flops 1000 | bytes 1000 | tf_op jit(solution)/shard_map/pack/pallas_call | solution.py:151
  24.1 35.8 %all-to-all-done.1 = bf16[64,24,1024]{2,1,0:T(8,128)(2,1)} async-done(((bf16[64,24,1024]{2,1,0:T(8,128)(2,1)}), bf16[64,24,1024]{2,1,0:T(8,128)(2,1)}, u32[]{:S(2)}, u32[]{:S(2)}) %all-to-all-start.1) | async-done | bytes 3145760 | tf_op jit(solution)/shard_map/all_to_all | solution.py:244
  59.9 9.5 %all-to-all-start = ((bf16[64,24,1024]{2,1,0:T(8,128)(2,1)}), bf16[64,24,1024]{2,1,0:T(8,128)(2,1)}, u32[]{:S(2)}, u32[]{:S(2)}) async-start(bf16[64,24,1024]{2,1,0:T(8,128)(2,1)} %bitcast.1), calls=%async_computation | async-start | bytes 6291456 | tf_op jit(solution)/shard_map/all_to_all | solution.py:244
  69.4 0.2 fusion.2
  69.6 10.9 %first_hidden.2 = (bf16[384,768]{1,0:T(8,128)(2,1)S(1)}, bf16[384,4096]{1,0:T(8,128)(2,1)S(1)}) custom-call(bf16[384,384]{1,0:T(8,128)(2,1)S(1)} %get-tuple-element.32.order, bf16[1536,1024]{1,0:T(8,128)(2,1)} %bitcast.4.x, bf16[1,4096,768]{2,1,0:T(8,128)(2,1)} %gate.3, bf16[1,4096,768]{2,1,0:T(8,128)(2,1)} %up.3), custom_call_target="tpu_custom_call" | custom-call | flops 1000 | bytes 1000 | tf_op jit(solution)/shard_map/first_hidden/pallas_call | solution.py:73
  80.5 0.0 collective-permute-done.gate
  80.5 0.0 collective-permute-done.1.up
  80.5 8.3 %hidden.2.act_b = bf16[384,768]{1,0:T(8,128)(2,1)S(1)} custom-call(bf16[384,4096]{1,0:T(8,128)(2,1)S(1)} %get-tuple-element.17.x, bf16[1,4096,768]{2,1,0:T(8,128)(2,1)} %collective-permute-done.gate, bf16[1,4096,768]{2,1,0:T(8,128)(2,1)} %collective-permute-done.1.up), custom_call_target="tpu_custom_call" | custom-call | flops 1000 | bytes 1000 | tf_op jit(solution)/shard_map/hidden/pallas_call | solution.py:64
  88.9 0.0 collective-permute-done.2.w_b
  88.9 13.5 %down.2 = bf16[1536,1024]{1,0:T(8,128)(2,1)} custom-call(bf16[384,384]{1,0:T(8,128)(2,1)S(1)} %get-tuple-element.31.order_t, bf16[384,768]{1,0:T(8,128)(2,1)S(1)} %get-tuple-element.16.act_a, bf16[384,768]{1,0:T(8,128)(2,1)S(1)} %hidden.2.act_b, bf16[1,768,4096]{2,1,0:T(8,128)(2,1)} %w_a.3, bf16[1,768,4096]{2,1,0:T(8,128)(2,1)} %collective-permute-done.2.w_b), custom_call_target="tpu_custom_call" | custom-call | flops 1000 | bytes 1000 | tf_op jit(solution)/shard_map/down/pallas_call | solution.py:112
  102.4 4.7 %all-to-all-done = bf16[64,24,1024]{2,1,0:T(8,128)(2,1)} async-done(((bf16[64,24,1024]{2,1,0:T(8,128)(2,1)}), bf16[64,24,1024]{2,1,0:T(8,128)(2,1)}, u32[]{:S(2)}, u32[]{:S(2)}) %all-to-all-start) | async-done | bytes 3145760 | tf_op jit(solution)/shard_map/all_to_all | solution.py:244
  107.1 9.6 %all-to-all-start.2 = ((bf16[64,24,1024]{2,1,0:T(8,128)(2,1)}), bf16[64,24,1024]{2,1,0:T(8,128)(2,1)}, u32[]{:S(2)}, u32[]{:S(2)}) async-start(bf16[64,24,1024]{2,1,0:T(8,128)(2,1)} %bitcast.5), calls=%async_computation.2 | async-start | bytes 6291456 | tf_op jit(solution)/shard_map/all_to_all | solution.py:244
  116.7 10.9 %first_hidden.3 = (bf16[384,768]{1,0:T(8,128)(2,1)S(1)}, bf16[384,4096]{1,0:T(8,128)(2,1)S(1)}) custom-call(bf16[384,384]{1,0:T(8,128)(2,1)S(1)} %get-tuple-element.32.order, bf16[1536,1024]{1,0:T(8,128)(2,1)} %bitcast.2.x, bf16[1,4096,768]{2,1,0:T(8,128)(2,1)} %gate.3, bf16[1,4096,768]{2,1,0:T(8,128)(2,1)} %up.3), custom_call_target="tpu_custom_call" | custom-call | flops 1000 | bytes 1000 | tf_op jit(solution)/shard_map/first_hidden/pallas_call | solution.py:73
  127.6 8.3 %hidden.3.act_b = bf16[384,768]{1,0:T(8,128)(2,1)S(1)} custom-call(bf16[384,4096]{1,0:T(8,128)(2,1)S(1)} %get-tuple-element.21.x, bf16[1,4096,768]{2,1,0:T(8,128)(2,1)} %collective-permute-done.gate, bf16[1,4096,768]{2,1,0:T(8,128)(2,1)} %collective-permute-done.1.up), custom_call_target="tpu_custom_call" | custom-call | flops 1000 | bytes 1000 | tf_op jit(solution)/shard_map/hidden/pallas_call | solution.py:64
  135.9 13.5 %down.3 = bf16[1536,1024]{1,0:T(8,128)(2,1)} custom-call(bf16[384,384]{1,0:T(8,128)(2,1)S(1)} %get-tuple-element.31.order_t, bf16[384,768]{1,0:T(8,128)(2,1)S(1)} %get-tuple-element.20.act_a, bf16[384,768]{1,0:T(8,128)(2,1)S(1)} %hidden.3.act_b, bf16[1,768,4096]{2,1,0:T(8,128)(2,1)} %w_a.3, bf16[1,768,4096]{2,1,0:T(8,128)(2,1)} %collective-permute-done.2.w_b), custom_call_target="tpu_custom_call" | custom-call | flops 1000 | bytes 1000 | tf_op jit(solution)/shard_map/down/pallas_call | solution.py:112
  149.5 5.2 %all-to-all-done.2 = bf16[64,24,1024]{2,1,0:T(8,128)(2,1)} async-done(((bf16[64,24,1024]{2,1,0:T(8,128)(2,1)}), bf16[64,24,1024]{2,1,0:T(8,128)(2,1)}, u32[]{:S(2)}, u32[]{:S(2)}) %all-to-all-start.2) | async-done | bytes 3145760 | tf_op jit(solution)/shard_map/all_to_all | solution.py:244
  154.6 9.2 %all-to-all-start.3 = ((bf16[64,24,1024]{2,1,0:T(8,128)(2,1)}), bf16[64,24,1024]{2,1,0:T(8,128)(2,1)}, u32[]{:S(2)}, u32[]{:S(2)}) async-start(bf16[64,24,1024]{2,1,0:T(8,128)(2,1)} %bitcast.7), calls=%async_computation.3 | async-start | bytes 6291456 | tf_op jit(solution)/shard_map/all_to_all | solution.py:244
  163.9 0.0 copy-done.3
  163.9 0.0 copy-done.2
  164.1 0.1 broadcast_in_dim.95
  164.1 0.2 copy.17
  164.4 0.1 eq.145
  164.4 0.2 copy.16
  164.6 0.1 eq.151
  164.8 0.1 eq.147
  164.9 0.1 compare_select_fusion
  165.0 0.2 broadcast_in_dim.97.before
  165.3 5.3 %combine.2.before = f32[128,4096]{1,0:T(8,128)S(1)} custom-call(bf16[384,384]{1,0:T(8,128)(2,1)S(1)} %get-tuple-element.32.order, bf16[256,384]{1,0:T(8,128)(2,1)S(1)} %get-tuple-element.28.placed, bf16[1536,1024]{1,0:T(8,128)(2,1)} %bitcast.6.back, f32[128,4096]{1,0:T(8,128)S(1)} %broadcast_in_dim.97.before), custom_call_target="tpu_custom_call" | custom-call | flops 1000 | bytes 1000 | tf_op jit(solution)/shard_map/combine/pallas_call | solution.py:191
  170.6 31.0 %all-to-all-done.3 = bf16[64,24,1024]{2,1,0:T(8,128)(2,1)} async-done(((bf16[64,24,1024]{2,1,0:T(8,128)(2,1)}), bf16[64,24,1024]{2,1,0:T(8,128)(2,1)}, u32[]{:S(2)}, u32[]{:S(2)}) %all-to-all-start.3) | async-done | bytes 3145760 | tf_op jit(solution)/shard_map/all_to_all | solution.py:244
  201.6 5.3 %combine.3 = bf16[128,4096]{1,0:T(8,128)(2,1)S(1)} custom-call(bf16[384,384]{1,0:T(8,128)(2,1)S(1)} %get-tuple-element.32.order, bf16[256,384]{1,0:T(8,128)(2,1)S(1)} %get-tuple-element.24.placed, bf16[1536,1024]{1,0:T(8,128)(2,1)} %bitcast.8.back, f32[128,4096]{1,0:T(8,128)S(1)} %combine.2.before), custom_call_target="tpu_custom_call" | custom-call | flops 1000 | bytes 1000 | tf_op jit(solution)/shard_map/combine/pallas_call | solution.py:191
  206.9 2.9 %collective-permute-start.3 = (bf16[128,4096]{1,0:T(8,128)(2,1)S(1)}, bf16[128,4096]{1,0:T(8,128)(2,1)S(1)}, u32[]{:S(2)}, u32[]{:S(2)}) collective-permute-start(bf16[128,4096]{1,0:T(8,128)(2,1)S(1)} %combine.3), channel_id=1, source_target_pairs={{0,64},{64,0},{1,65},{65,1},{2,66},{66,2},{3,67},{67,3},{4,68},{68... | collective-permute-start | bytes 3145736 | tf_op jit(solution)/shard_map/ppermute | solution.py:269
  209.9 2.3 %collective-permute-done.3 = bf16[128,4096]{1,0:T(8,128)(2,1)S(1)} collective-permute-done((bf16[128,4096]{1,0:T(8,128)(2,1)S(1)}, bf16[128,4096]{1,0:T(8,128)(2,1)S(1)}, u32[]{:S(2)}, u32[]{:S(2)}) %collective-permute-start.3) | collective-permute-done | bytes 1048608 | tf_op jit(solution)/shard_map/ppermute | solution.py:269
  212.2 1.2 add_convert_fusion
  (21 shorter events, 0.3 us)
Async XLA Ops:
  0.0 80.5 %collective-permute-start = (bf16[1,4096,768]{2,1,0:T(8,128)(2,1)}, bf16[1,4096,768]{2,1,0:T(8,128)(2,1)}, u32[]{:S(2)}, u32[]{:S(2)}) collective-permute-start(bf16[1,4096,768]{2,1,0:T(8,128)(2,1)} %gate.3), channel_id=1, source_target_pairs={{0,64},{64,0},{1,65},{65,1},{2,66},{66,2},{3,67},{67,3},{4,68},{68... | collective-permute-start | bytes 18874376 | tf_op jit(solution)/shard_map/ppermute | solution.py:233
  1.4 79.1 %collective-permute-start.1 = (bf16[1,4096,768]{2,1,0:T(8,128)(2,1)}, bf16[1,4096,768]{2,1,0:T(8,128)(2,1)}, u32[]{:S(2)}, u32[]{:S(2)}) collective-permute-start(bf16[1,4096,768]{2,1,0:T(8,128)(2,1)} %up.3), channel_id=1, source_target_pairs={{0,64},{64,0},{1,65},{65,1},{2,66},{66,2},{3,67},{67,3},{4,68},{68... | collective-permute-start | bytes 18874376 | tf_op jit(solution)/shard_map/ppermute | solution.py:234
  1.4 87.4 %collective-permute-start.2 = (bf16[1,768,4096]{2,1,0:T(8,128)(2,1)}, bf16[1,768,4096]{2,1,0:T(8,128)(2,1)}, u32[]{:S(2)}, u32[]{:S(2)}) collective-permute-start(bf16[1,768,4096]{2,1,0:T(8,128)(2,1)} %w_a.3), channel_id=1, source_target_pairs={{0,64},{64,0},{1,65},{65,1},{2,66},{66,2},{3,67},{67,3},{4,68},{68... | collective-permute-start | bytes 18874376 | tf_op jit(solution)/shard_map/ppermute | solution.py:235
  3.3 1.2 copy-start
  8.5 11.7 %copy-start.1 = (bf16[128,4096]{1,0:T(8,128)(2,1)S(1)}, bf16[128,4096]{1,0:T(8,128)(2,1)}, u32[]{:S(2)}) copy-start(bf16[128,4096]{1,0:T(8,128)(2,1)} %tokens.3) | copy-start | bytes 3145732
  8.5 51.5 %all-to-all-start.1 = ((bf16[64,24,1024]{2,1,0:T(8,128)(2,1)}), bf16[64,24,1024]{2,1,0:T(8,128)(2,1)}, u32[]{:S(2)}, u32[]{:S(2)}) async-start(bf16[64,24,1024]{2,1,0:T(8,128)(2,1)} %bitcast.3), calls=%async_computation.1 | async-start | bytes 6291456 | tf_op jit(solution)/shard_map/all_to_all | solution.py:244
  59.9 47.2 %all-to-all-start = ((bf16[64,24,1024]{2,1,0:T(8,128)(2,1)}), bf16[64,24,1024]{2,1,0:T(8,128)(2,1)}, u32[]{:S(2)}, u32[]{:S(2)}) async-start(bf16[64,24,1024]{2,1,0:T(8,128)(2,1)} %bitcast.1), calls=%async_computation | async-start | bytes 6291456 | tf_op jit(solution)/shard_map/all_to_all | solution.py:244
  107.1 47.5 %all-to-all-start.2 = ((bf16[64,24,1024]{2,1,0:T(8,128)(2,1)}), bf16[64,24,1024]{2,1,0:T(8,128)(2,1)}, u32[]{:S(2)}, u32[]{:S(2)}) async-start(bf16[64,24,1024]{2,1,0:T(8,128)(2,1)} %bitcast.5), calls=%async_computation.2 | async-start | bytes 6291456 | tf_op jit(solution)/shard_map/all_to_all | solution.py:244
  154.6 9.3 %copy-start.3 = (f32[128,8]{0,1:T(8,128)S(1)}, f32[128,8]{0,1:T(8,128)}, u32[]{:S(2)}) copy-start(f32[128,8]{0,1:T(8,128)} %param.8) | copy-start | bytes 12292
  154.6 9.3 %copy-start.2 = (s32[128,8]{0,1:T(8,128)S(1)}, s32[128,8]{0,1:T(8,128)}, u32[]{:S(2)}) copy-start(s32[128,8]{0,1:T(8,128)} %param.7) | copy-start | bytes 12292
  154.6 47.0 %all-to-all-start.3 = ((bf16[64,24,1024]{2,1,0:T(8,128)(2,1)}), bf16[64,24,1024]{2,1,0:T(8,128)(2,1)}, u32[]{:S(2)}, u32[]{:S(2)}) async-start(bf16[64,24,1024]{2,1,0:T(8,128)(2,1)} %bitcast.7), calls=%async_computation.3 | async-start | bytes 6291456 | tf_op jit(solution)/shard_map/all_to_all | solution.py:244
  206.9 5.2 %collective-permute-start.3 = (bf16[128,4096]{1,0:T(8,128)(2,1)S(1)}, bf16[128,4096]{1,0:T(8,128)(2,1)S(1)}, u32[]{:S(2)}, u32[]{:S(2)}) collective-permute-start(bf16[128,4096]{1,0:T(8,128)(2,1)S(1)} %combine.3), channel_id=1, source_target_pairs={{0,64},{64,0},{1,65},{65,1},{2,66},{66,2},{3,67},{67,3},{4,68},{68... | collective-permute-start | bytes 3145736 | tf_op jit(solution)/shard_map/ppermute | solution.py:269

commit v3 on v2

--- a/solution.py
+++ b/solution.py
@@ -7,6 +7,7 @@
 
 SLOTS, QUARTERS = 6, 4
 GROUP = 16
+COMBINE_STEPS = 2
 SWAP = ((0, 1), (1, 0))
 VMEM = 48 * 2**20
 COST = pl.CostEstimate(flops=1000, bytes_accessed=1000, transcendentals=0)
@@ -141,7 +142,7 @@
 def pack(first, rank, tokens):
     n, rows = rank.shape
     quarter = tokens.shape[1] // QUARTERS
-    step = 16
+    step = 32
     part = SLOTS * QUARTERS
     at = jnp.arange(step * part, dtype=jnp.int32)
     wide = (step * part, rows)
@@ -167,39 +168,40 @@
 
 
 def combine_kernel(order, placed, back, before, out, lines):
-    size, quarter = back.shape
+    quarter = back.shape[1]
     rows = out.shape[0]
-    count = size // QUARTERS
+    count = back.shape[0] // QUARTERS
     step = pl.program_id(0)
-    y = dot(order[...], back[...]).astype(back.dtype)
-    for q in range(QUARTERS):
-        lines[
-            pl.ds(pl.multiple_of(step * count, count), count), q * quarter : (q + 1) * quarter
-        ] = y[q * count : (q + 1) * count]
+    order_rows(order, back, lines.at[step])
 
     @pl.when(step == pl.num_programs(0) - 1)
     def _():
         for q in range(QUARTERS):
             here = slice(q * quarter, (q + 1) * quarter)
-            both = dot(placed[...], lines[:, here])
-            out[:, here] = (both[:rows] + both[rows:] + before[:, here]).astype(out.dtype)
+            both = before[:, here]
+            for g in range(lines.shape[0]):
+                product = dot(placed[:, g * count : (g + 1) * count], lines[g, :, here])
+                both = both + product[:rows] + product[rows:]
+            out[:, here] = both.astype(out.dtype)
 
 
 def combine(order, placed, back, before, kind):
-    size = order.shape[0]
-    quarter = back.shape[1]
+    m, quarter = back.shape
+    steps = COMBINE_STEPS
     return pl.pallas_call(
         combine_kernel,
         out_shape=jax.ShapeDtypeStruct(before.shape, kind),
-        grid=(back.shape[0] // size,),
+        grid=(steps,),
         in_specs=[
             whole(order.shape),
             whole(placed.shape),
-            pl.BlockSpec((size, quarter), lambda i: (i, 0)),
+            pl.BlockSpec((m // steps, quarter), lambda i: (i, 0)),
             whole(before.shape),
         ],
         out_specs=whole(before.shape),
-        scratch_shapes=[pltpu.VMEM((placed.shape[1], QUARTERS * quarter), back.dtype)],
+        scratch_shapes=[
+            pltpu.VMEM((steps, m // QUARTERS // steps, QUARTERS * quarter), back.dtype)
+        ],
         name="combine",
         **params(),
     )(order, placed, back, before)

time: 214 us -> 213 us (level)
  Pallas kernels: 83.9 us -> 81.6 us
  transfers between devices with their start and end apart: 8 -> 8, of which waited for: 5 -> 5; matrix products, arithmetic and copies ran while one was open for 1% -> 1% of each run, Pallas kernels for 37% -> 36%
where the time goes in v3:
time: 213 us; the launch traced here: 212 us
  Pallas kernels  81.6 us (38%)
  waiting for transfers between devices  80.1 us (38%)
  starting transfers between devices  44.8 us (21%)
  local copies, waits for them, and re-layouts  2.7 us (1%)
  other arithmetic  2.6 us (1%)
    all_to_all x4, waiting for transfers between devices, exchange(): a = lax.all_to_all(a, 'dev', split_axis=0, concat_axis=0, tiled=True)  77.8 us
    all_to_all x4, starting transfers between devices, exchange(): a = lax.all_to_all(a, 'dev', split_axis=0, concat_axis=0, tiled=True)  39.9 us
    pallas_call x2, Pallas kernels, down(): pl.pallas_call(down_kernel, out_shape=jax.ShapeDtypeStruct((m * QUARTERS,...  27 us
    pallas_call x2, Pallas kernels, hidden_units(): pl.pallas_call(first_hidden_kernel, out_shape=[act, jax.ShapeDtypeStruct(...  21.8 us
    pallas_call x2, Pallas kernels, hidden_units(): pl.pallas_call(hidden_kernel, out_shape=act, grid=(ff // block,), in_spec...  16.6 us
    pallas_call x2, Pallas kernels, combine(): pl.pallas_call(combine_kernel, out_shape=jax.ShapeDtypeStruct(before.shap...  9.29 us
    pallas_call x2, Pallas kernels, pack(): pl.pallas_call(pack_kernel, out_shape=jax.ShapeDtypeStruct((n * part, qua...  6.84 us
  transfers between devices with their start and end apart: 8, of which 5 were waited for; matrix products, arithmetic and copies ran while one was open for 1% of the time, Pallas kernels for 36%

profile of v3, /device:TPU:1, one launch (start us, length us, event | category | flops | bytes accessed | tf_op | source)
XLA Modules:
  0.0 212.3 jit_solution(16085458519983377073)
XLA Ops:
  0.0 1.4 collective-permute-start
  1.4 0.0 collective-permute-start.1
  1.4 0.5 collective-permute-start.2
  2.0 0.2 fusion.3.expand
  2.2 0.7 fusion.4
  2.9 0.2 fusion
  3.1 0.2 broadcast_in_dim.47.row_quarter
  3.3 0.2 broadcast_in_dim.55.row_slot
  3.5 0.0 copy-start
  3.5 1.2 copy-done
  4.7 3.4 %pack.3 = bf16[1536,1024]{1,0:T(8,128)(2,1)} custom-call(bf16[768,32]{1,0:T(8,128)(2,1)S(1)} %fusion.3.expand, f32[768,128]{1,0:T(8,128)S(1)} %broadcast_in_dim.55.row_slot, f32[768,128]{1,0:T(8,128)S(1)} %broadcast_in_dim.47.row_quarter, bf16[64,128]{1,0:T(8,128)(2,1)S(1)} %convert_bitcast_fusion.rank, bf16[128,4096]{1,0:T(8,128)(2,1)S(1)} %copy-done), custom_call_target="tpu_custom_call" | custom-call | flops 1000 | bytes 1000 | tf_op jit(solution)/shard_map/pack/pallas_call | solution.py:152
  8.1 0.0 copy-start.1
  8.1 11.6 %all-to-all-start.1 = ((bf16[64,24,1024]{2,1,0:T(8,128)(2,1)}), bf16[64,24,1024]{2,1,0:T(8,128)(2,1)}, u32[]{:S(2)}, u32[]{:S(2)}) async-start(bf16[64,24,1024]{2,1,0:T(8,128)(2,1)} %bitcast.3), calls=%async_computation.1 | async-start | bytes 6291456 | tf_op jit(solution)/shard_map/all_to_all | solution.py:246
  19.7 0.2 broadcast_in_dim.46.row_slot
  19.9 0.0 copy-done.1
  19.9 3.4 %pack.2 = bf16[1536,1024]{1,0:T(8,128)(2,1)} custom-call(bf16[768,32]{1,0:T(8,128)(2,1)S(1)} %fusion.3.expand, f32[768,128]{1,0:T(8,128)S(1)} %broadcast_in_dim.46.row_slot, f32[768,128]{1,0:T(8,128)S(1)} %broadcast_in_dim.47.row_quarter, bf16[64,128]{1,0:T(8,128)(2,1)S(1)} %convert_bitcast_fusion.rank, bf16[128,4096]{1,0:T(8,128)(2,1)S(1)} %copy-done.1), custom_call_target="tpu_custom_call" | custom-call | flops 1000 | bytes 1000 | tf_op jit(solution)/shard_map/pack/pallas_call | solution.py:152
  23.3 36.2 %all-to-all-done.1 = bf16[64,24,1024]{2,1,0:T(8,128)(2,1)} async-done(((bf16[64,24,1024]{2,1,0:T(8,128)(2,1)}), bf16[64,24,1024]{2,1,0:T(8,128)(2,1)}, u32[]{:S(2)}, u32[]{:S(2)}) %all-to-all-start.1) | async-done | bytes 3145760 | tf_op jit(solution)/shard_map/all_to_all | solution.py:246
  59.6 9.5 %all-to-all-start = ((bf16[64,24,1024]{2,1,0:T(8,128)(2,1)}), bf16[64,24,1024]{2,1,0:T(8,128)(2,1)}, u32[]{:S(2)}, u32[]{:S(2)}) async-start(bf16[64,24,1024]{2,1,0:T(8,128)(2,1)} %bitcast.1), calls=%async_computation | async-start | bytes 6291456 | tf_op jit(solution)/shard_map/all_to_all | solution.py:246
  69.1 0.2 fusion.2
  69.2 10.9 %first_hidden.2 = (bf16[384,768]{1,0:T(8,128)(2,1)S(1)}, bf16[384,4096]{1,0:T(8,128)(2,1)S(1)}) custom-call(bf16[384,384]{1,0:T(8,128)(2,1)S(1)} %get-tuple-element.32.order, bf16[1536,1024]{1,0:T(8,128)(2,1)} %bitcast.4.x, bf16[1,4096,768]{2,1,0:T(8,128)(2,1)} %gate.3, bf16[1,4096,768]{2,1,0:T(8,128)(2,1)} %up.3), custom_call_target="tpu_custom_call" | custom-call | flops 1000 | bytes 1000 | tf_op jit(solution)/shard_map/first_hidden/pallas_call | solution.py:74
  80.1 0.0 collective-permute-done.gate
  80.2 0.0 collective-permute-done.1.up
  80.2 8.3 %hidden.2.act_b = bf16[384,768]{1,0:T(8,128)(2,1)S(1)} custom-call(bf16[384,4096]{1,0:T(8,128)(2,1)S(1)} %get-tuple-element.17.x, bf16[1,4096,768]{2,1,0:T(8,128)(2,1)} %collective-permute-done.gate, bf16[1,4096,768]{2,1,0:T(8,128)(2,1)} %collective-permute-done.1.up), custom_call_target="tpu_custom_call" | custom-call | flops 1000 | bytes 1000 | tf_op jit(solution)/shard_map/hidden/pallas_call | solution.py:65
  88.5 0.0 collective-permute-done.2.w_b
  88.5 13.5 %down.2 = bf16[1536,1024]{1,0:T(8,128)(2,1)} custom-call(bf16[384,384]{1,0:T(8,128)(2,1)S(1)} %get-tuple-element.31.order_t, bf16[384,768]{1,0:T(8,128)(2,1)S(1)} %get-tuple-element.16.act_a, bf16[384,768]{1,0:T(8,128)(2,1)S(1)} %hidden.2.act_b, bf16[1,768,4096]{2,1,0:T(8,128)(2,1)} %w_a.3, bf16[1,768,4096]{2,1,0:T(8,128)(2,1)} %collective-permute-done.2.w_b), custom_call_target="tpu_custom_call" | custom-call | flops 1000 | bytes 1000 | tf_op jit(solution)/shard_map/down/pallas_call | solution.py:113
  102.0 4.7 %all-to-all-done = bf16[64,24,1024]{2,1,0:T(8,128)(2,1)} async-done(((bf16[64,24,1024]{2,1,0:T(8,128)(2,1)}), bf16[64,24,1024]{2,1,0:T(8,128)(2,1)}, u32[]{:S(2)}, u32[]{:S(2)}) %all-to-all-start) | async-done | bytes 3145760 | tf_op jit(solution)/shard_map/all_to_all | solution.py:246
  106.7 9.6 %all-to-all-start.2 = ((bf16[64,24,1024]{2,1,0:T(8,128)(2,1)}), bf16[64,24,1024]{2,1,0:T(8,128)(2,1)}, u32[]{:S(2)}, u32[]{:S(2)}) async-start(bf16[64,24,1024]{2,1,0:T(8,128)(2,1)} %bitcast.5), calls=%async_computation.2 | async-start | bytes 6291456 | tf_op jit(solution)/shard_map/all_to_all | solution.py:246
  116.3 10.9 %first_hidden.3 = (bf16[384,768]{1,0:T(8,128)(2,1)S(1)}, bf16[384,4096]{1,0:T(8,128)(2,1)S(1)}) custom-call(bf16[384,384]{1,0:T(8,128)(2,1)S(1)} %get-tuple-element.32.order, bf16[1536,1024]{1,0:T(8,128)(2,1)} %bitcast.2.x, bf16[1,4096,768]{2,1,0:T(8,128)(2,1)} %gate.3, bf16[1,4096,768]{2,1,0:T(8,128)(2,1)} %up.3), custom_call_target="tpu_custom_call" | custom-call | flops 1000 | bytes 1000 | tf_op jit(solution)/shard_map/first_hidden/pallas_call | solution.py:74
  127.2 8.3 %hidden.3.act_b = bf16[384,768]{1,0:T(8,128)(2,1)S(1)} custom-call(bf16[384,4096]{1,0:T(8,128)(2,1)S(1)} %get-tuple-element.21.x, bf16[1,4096,768]{2,1,0:T(8,128)(2,1)} %collective-permute-done.gate, bf16[1,4096,768]{2,1,0:T(8,128)(2,1)} %collective-permute-done.1.up), custom_call_target="tpu_custom_call" | custom-call | flops 1000 | bytes 1000 | tf_op jit(solution)/shard_map/hidden/pallas_call | solution.py:65
  135.6 13.5 %down.3 = bf16[1536,1024]{1,0:T(8,128)(2,1)} custom-call(bf16[384,384]{1,0:T(8,128)(2,1)S(1)} %get-tuple-element.31.order_t, bf16[384,768]{1,0:T(8,128)(2,1)S(1)} %get-tuple-element.20.act_a, bf16[384,768]{1,0:T(8,128)(2,1)S(1)} %hidden.3.act_b, bf16[1,768,4096]{2,1,0:T(8,128)(2,1)} %w_a.3, bf16[1,768,4096]{2,1,0:T(8,128)(2,1)} %collective-permute-done.2.w_b), custom_call_target="tpu_custom_call" | custom-call | flops 1000 | bytes 1000 | tf_op jit(solution)/shard_map/down/pallas_call | solution.py:113
  149.1 5.2 %all-to-all-done.2 = bf16[64,24,1024]{2,1,0:T(8,128)(2,1)} async-done(((bf16[64,24,1024]{2,1,0:T(8,128)(2,1)}), bf16[64,24,1024]{2,1,0:T(8,128)(2,1)}, u32[]{:S(2)}, u32[]{:S(2)}) %all-to-all-start.2) | async-done | bytes 3145760 | tf_op jit(solution)/shard_map/all_to_all | solution.py:246
  154.3 9.2 %all-to-all-start.3 = ((bf16[64,24,1024]{2,1,0:T(8,128)(2,1)}), bf16[64,24,1024]{2,1,0:T(8,128)(2,1)}, u32[]{:S(2)}, u32[]{:S(2)}) async-start(bf16[64,24,1024]{2,1,0:T(8,128)(2,1)} %bitcast.7), calls=%async_computation.3 | async-start | bytes 6291456 | tf_op jit(solution)/shard_map/all_to_all | solution.py:246
  163.5 0.0 copy-done.3
  163.6 0.0 copy-done.2
  163.7 0.1 broadcast_in_dim.95
  163.8 0.2 copy.17
  164.0 0.1 eq.146
  164.0 0.2 copy.16
  164.2 0.1 eq.152
  164.4 0.1 eq.148
  164.5 0.1 compare_select_fusion
  164.7 0.2 broadcast_in_dim.97.before
  164.9 4.7 %combine.2.before = f32[128,4096]{1,0:T(8,128)S(1)} custom-call(bf16[384,384]{1,0:T(8,128)(2,1)S(1)} %get-tuple-element.32.order, bf16[256,384]{1,0:T(8,128)(2,1)S(1)} %get-tuple-element.28.placed, bf16[1536,1024]{1,0:T(8,128)(2,1)} %bitcast.6.back, f32[128,4096]{1,0:T(8,128)S(1)} %broadcast_in_dim.97.before), custom_call_target="tpu_custom_call" | custom-call | flops 1000 | bytes 1000 | tf_op jit(solution)/shard_map/combine/pallas_call | solution.py:191
  169.5 31.7 %all-to-all-done.3 = bf16[64,24,1024]{2,1,0:T(8,128)(2,1)} async-done(((bf16[64,24,1024]{2,1,0:T(8,128)(2,1)}), bf16[64,24,1024]{2,1,0:T(8,128)(2,1)}, u32[]{:S(2)}, u32[]{:S(2)}) %all-to-all-start.3) | async-done | bytes 3145760 | tf_op jit(solution)/shard_map/all_to_all | solution.py:246
  201.2 4.6 %combine.3 = bf16[128,4096]{1,0:T(8,128)(2,1)S(1)} custom-call(bf16[384,384]{1,0:T(8,128)(2,1)S(1)} %get-tuple-element.32.order, bf16[256,384]{1,0:T(8,128)(2,1)S(1)} %get-tuple-element.24.placed, bf16[1536,1024]{1,0:T(8,128)(2,1)} %bitcast.8.back, f32[128,4096]{1,0:T(8,128)S(1)} %combine.2.before), custom_call_target="tpu_custom_call" | custom-call | flops 1000 | bytes 1000 | tf_op jit(solution)/shard_map/combine/pallas_call | solution.py:191
  205.9 2.9 %collective-permute-start.3 = (bf16[128,4096]{1,0:T(8,128)(2,1)S(1)}, bf16[128,4096]{1,0:T(8,128)(2,1)S(1)}, u32[]{:S(2)}, u32[]{:S(2)}) collective-permute-start(bf16[128,4096]{1,0:T(8,128)(2,1)S(1)} %combine.3), channel_id=1, source_target_pairs={{0,64},{64,0},{1,65},{65,1},{2,66},{66,2},{3,67},{67,3},{4,68},{68... | collective-permute-start | bytes 3145736 | tf_op jit(solution)/shard_map/ppermute | solution.py:271
  208.8 2.3 %collective-permute-done.3 = bf16[128,4096]{1,0:T(8,128)(2,1)S(1)} collective-permute-done((bf16[128,4096]{1,0:T(8,128)(2,1)S(1)}, bf16[128,4096]{1,0:T(8,128)(2,1)S(1)}, u32[]{:S(2)}, u32[]{:S(2)}) %collective-permute-start.3) | collective-permute-done | bytes 1048608 | tf_op jit(solution)/shard_map/ppermute | solution.py:271
  211.1 1.2 add_convert_fusion
  (21 shorter events, 0.3 us)
Async XLA Ops:
  0.0 80.1 %collective-permute-start = (bf16[1,4096,768]{2,1,0:T(8,128)(2,1)}, bf16[1,4096,768]{2,1,0:T(8,128)(2,1)}, u32[]{:S(2)}, u32[]{:S(2)}) collective-permute-start(bf16[1,4096,768]{2,1,0:T(8,128)(2,1)} %gate.3), channel_id=1, source_target_pairs={{0,64},{64,0},{1,65},{65,1},{2,66},{66,2},{3,67},{67,3},{4,68},{68... | collective-permute-start | bytes 18874376 | tf_op jit(solution)/shard_map/ppermute | solution.py:235
  1.4 78.7 %collective-permute-start.1 = (bf16[1,4096,768]{2,1,0:T(8,128)(2,1)}, bf16[1,4096,768]{2,1,0:T(8,128)(2,1)}, u32[]{:S(2)}, u32[]{:S(2)}) collective-permute-start(bf16[1,4096,768]{2,1,0:T(8,128)(2,1)} %up.3), channel_id=1, source_target_pairs={{0,64},{64,0},{1,65},{65,1},{2,66},{66,2},{3,67},{67,3},{4,68},{68... | collective-permute-start | bytes 18874376 | tf_op jit(solution)/shard_map/ppermute | solution.py:236
  1.4 87.1 %collective-permute-start.2 = (bf16[1,768,4096]{2,1,0:T(8,128)(2,1)}, bf16[1,768,4096]{2,1,0:T(8,128)(2,1)}, u32[]{:S(2)}, u32[]{:S(2)}) collective-permute-start(bf16[1,768,4096]{2,1,0:T(8,128)(2,1)} %w_a.3), channel_id=1, source_target_pairs={{0,64},{64,0},{1,65},{65,1},{2,66},{66,2},{3,67},{67,3},{4,68},{68... | collective-permute-start | bytes 18874376 | tf_op jit(solution)/shard_map/ppermute | solution.py:237
  3.5 1.2 copy-start
  8.1 11.8 %copy-start.1 = (bf16[128,4096]{1,0:T(8,128)(2,1)S(1)}, bf16[128,4096]{1,0:T(8,128)(2,1)}, u32[]{:S(2)}) copy-start(bf16[128,4096]{1,0:T(8,128)(2,1)} %tokens.3) | copy-start | bytes 3145732
  8.1 51.5 %all-to-all-start.1 = ((bf16[64,24,1024]{2,1,0:T(8,128)(2,1)}), bf16[64,24,1024]{2,1,0:T(8,128)(2,1)}, u32[]{:S(2)}, u32[]{:S(2)}) async-start(bf16[64,24,1024]{2,1,0:T(8,128)(2,1)} %bitcast.3), calls=%async_computation.1 | async-start | bytes 6291456 | tf_op jit(solution)/shard_map/all_to_all | solution.py:246
  59.6 47.2 %all-to-all-start = ((bf16[64,24,1024]{2,1,0:T(8,128)(2,1)}), bf16[64,24,1024]{2,1,0:T(8,128)(2,1)}, u32[]{:S(2)}, u32[]{:S(2)}) async-start(bf16[64,24,1024]{2,1,0:T(8,128)(2,1)} %bitcast.1), calls=%async_computation | async-start | bytes 6291456 | tf_op jit(solution)/shard_map/all_to_all | solution.py:246
  106.7 47.5 %all-to-all-start.2 = ((bf16[64,24,1024]{2,1,0:T(8,128)(2,1)}), bf16[64,24,1024]{2,1,0:T(8,128)(2,1)}, u32[]{:S(2)}, u32[]{:S(2)}) async-start(bf16[64,24,1024]{2,1,0:T(8,128)(2,1)} %bitcast.5), calls=%async_computation.2 | async-start | bytes 6291456 | tf_op jit(solution)/shard_map/all_to_all | solution.py:246
  154.3 9.3 %copy-start.3 = (f32[128,8]{0,1:T(8,128)S(1)}, f32[128,8]{0,1:T(8,128)}, u32[]{:S(2)}) copy-start(f32[128,8]{0,1:T(8,128)} %param.8) | copy-start | bytes 12292
  154.3 9.3 %copy-start.2 = (s32[128,8]{0,1:T(8,128)S(1)}, s32[128,8]{0,1:T(8,128)}, u32[]{:S(2)}) copy-start(s32[128,8]{0,1:T(8,128)} %param.7) | copy-start | bytes 12292
  154.3 47.0 %all-to-all-start.3 = ((bf16[64,24,1024]{2,1,0:T(8,128)(2,1)}), bf16[64,24,1024]{2,1,0:T(8,128)(2,1)}, u32[]{:S(2)}, u32[]{:S(2)}) async-start(bf16[64,24,1024]{2,1,0:T(8,128)(2,1)} %bitcast.7), calls=%async_computation.3 | async-start | bytes 6291456 | tf_op jit(solution)/shard_map/all_to_all | solution.py:246
  205.9 5.2 %collective-permute-start.3 = (bf16[128,4096]{1,0:T(8,128)(2,1)S(1)}, bf16[128,4096]{1,0:T(8,128)(2,1)S(1)}, u32[]{:S(2)}, u32[]{:S(2)}) collective-permute-start(bf16[128,4096]{1,0:T(8,128)(2,1)S(1)} %combine.3), channel_id=1, source_target_pairs={{0,64},{64,0},{1,65},{65,1},{2,66},{66,2},{3,67},{67,3},{4,68},{68... | collective-permute-start | bytes 3145736 | tf_op jit(solution)/shard_map/ppermute | solution.py:271
